TPU v7x, 256 devices: a whole 4x4x8 slice. The times are simulated.
256 devices in a mesh: dp: 4 (over y_lo, core), ctx: 64 (over z, x, y_hi).
Axes of the slice: x: 4, y: 4 (y_hi: 2, y_lo: 2; y = y_hi * 2 + y_lo), z: 8, core: 2. Of those that a mesh axis runs over, the one named last changes fastest.
Arguments:
- queries: bfloat16 [4, 16384, 4096], P('dp', 'ctx'), may hold values from -130 to 130
- keys: bfloat16 [4, 16384, 1024], P('dp', 'ctx'), may hold values from -5 to 5
- values: bfloat16 [4, 16384, 1024], P('dp', 'ctx'), may hold values from -6 to 6
- out_grad: bfloat16 [4, 16384, 4096], P('dp', 'ctx'), may hold values from -6 to 6
- layer_input: bfloat16 [4, 16384, 4096], P('dp', 'ctx'), may hold values from -16 to 16
- doc_lengths: int32 [4, 64], P('dp'), may hold values from 1 to 512, 16384 in all within a row
Outputs:
- query_grad: bfloat16 [4, 16384, 4096], P('dp', 'ctx')
- key_grad: bfloat16 [4, 16384, 1024], P('dp', 'ctx')
- value_grad: bfloat16 [4, 16384, 1024], P('dp', 'ctx')
- value_weight_grad: float32 [4096, 1024], P(('dp', 'ctx'))
Inputs may be any that keep to these rules, and one draw needn't show every extreme that they name: `doc_lengths`: each sequence's lengths sum to 16384, and the longest document of each sequence has exactly 512 tokens.
All inputs are finite; a program needn't handle non-finite values.
Results may differ from a plain program's by a relative error of at most 0.029.
Values may be sent and summed in bfloat16 or wider, within the bound.
A program may use at most 128 MiB of HBM per device.

v0:
```python
import jax
import jax.numpy as jnp
from jax import lax
from jax.sharding import PartitionSpec as P

KVH = 8
HD = 128
REACH = 2
GROUP = 4


def shifted(block, axis, distance):
    devices = range(lax.axis_size(axis))
    route = [(i - distance, i) for i in devices if i - distance in devices]
    return lax.ppermute(block, axis, route)


def group_grads(group, carry, q_rows, k_window, v_window, do_rows, mask):
    dq_acc, dk_acc, dv_acc = carry
    scale = HD ** (-0.5)
    rows = q_rows.shape[0]
    q_group = lax.dynamic_slice_in_dim(q_rows, group * (GROUP * HD), GROUP * HD, 1).reshape(
        rows, GROUP, HD
    )
    do_group = lax.dynamic_slice_in_dim(do_rows, group * (GROUP * HD), GROUP * HD, 1).reshape(
        rows, GROUP, HD
    )
    k_group = lax.dynamic_slice_in_dim(k_window, group * HD, HD, 1)
    v_group = lax.dynamic_slice_in_dim(v_window, group * HD, HD, 1)
    scores = jnp.einsum("sed,wd->esw", q_group, k_group, preferred_element_type=jnp.float32) * scale
    live = mask[None]
    top = jnp.max(jnp.where(live, scores, -1e30), axis=-1, keepdims=True)
    total = jnp.sum(jnp.where(live, jnp.exp(scores - top), 0.0), axis=-1, keepdims=True)
    lse = top + jnp.log(total)
    probs = jnp.where(live, jnp.exp(scores - lse), 0.0)
    probs_b = probs.astype(jnp.bfloat16)
    attn_out = jnp.einsum("esw,wd->sed", probs_b, v_group, preferred_element_type=jnp.float32)
    delta = jnp.transpose(jnp.sum(do_group.astype(jnp.float32) * attn_out, axis=-1))[..., None]
    dprobs = jnp.einsum("sed,wd->esw", do_group, v_group, preferred_element_type=jnp.float32)
    dscores_b = (probs * (dprobs - delta)).astype(jnp.bfloat16)
    dq_group = (
        jnp.einsum("esw,wd->sed", dscores_b, k_group, preferred_element_type=jnp.float32) * scale
    )
    dk_group = (
        jnp.einsum("esw,sed->wd", dscores_b, q_group, preferred_element_type=jnp.float32) * scale
    )
    dv_group = jnp.einsum("esw,sed->wd", probs_b, do_group, preferred_element_type=jnp.float32)
    dq_acc = lax.dynamic_update_slice_in_dim(
        dq_acc, dq_group.reshape(rows, GROUP * HD), group * (GROUP * HD), 1
    )
    dk_acc = lax.dynamic_update_slice_in_dim(dk_acc, dk_group, group * HD, 1)
    dv_acc = lax.dynamic_update_slice_in_dim(dv_acc, dv_group, group * HD, 1)
    return (dq_acc, dk_acc, dv_acc)


def local(queries, keys, values, out_grad, layer_input, doc_lengths):
    q_rows = queries[0]
    k_rows = keys[0]
    v_rows = values[0]
    do_rows = out_grad[0]
    x_rows = layer_input[0]
    lengths = doc_lengths[0]
    rows = q_rows.shape[0]
    width = (REACH + 1) * rows
    here = lax.axis_index("ctx")
    ends = jnp.cumsum(lengths)
    starts = ends - lengths
    qpos = here * rows + jnp.arange(rows, dtype=jnp.int32)
    kpos = (here - REACH) * rows + jnp.arange(width, dtype=jnp.int32)
    qstart = jnp.max(jnp.where(starts[None, :] <= qpos[:, None], starts[None, :], 0), axis=1)
    mask = (kpos[None, :] <= qpos[:, None]) & (kpos[None, :] >= qstart[:, None])
    own_pair = jnp.stack((k_rows, v_rows))
    remote = [shifted(own_pair, "ctx", step) for step in range(1, REACH + 1)]
    ordered = [remote[REACH - 1 - index] for index in range(REACH)] + [own_pair]
    k_window = jnp.concatenate([pair[0] for pair in ordered], 0)
    v_window = jnp.concatenate([pair[1] for pair in ordered], 0)
    start_carry = (
        jnp.zeros((rows, q_rows.shape[1]), jnp.float32),
        jnp.zeros((width, k_rows.shape[1]), jnp.float32),
        jnp.zeros((width, k_rows.shape[1]), jnp.float32),
    )

    def loop_body(group, carry):
        return group_grads(group, carry, q_rows, k_window, v_window, do_rows, mask)

    dq_acc, dk_window, dv_window = lax.fori_loop(0, KVH, loop_body, start_carry)
    pieces = [
        jnp.stack(
            (
                dk_window[(REACH - step) * rows : (REACH - step + 1) * rows],
                dv_window[(REACH - step) * rows : (REACH - step + 1) * rows],
            )
        )
        for step in range(REACH + 1)
    ]
    summed = pieces[0]
    for step in range(1, REACH + 1):
        summed = summed + shifted(pieces[step], "ctx", -step)
    query_grad = dq_acc.astype(jnp.bfloat16)[None]
    key_grad = summed[0].astype(jnp.bfloat16)
    value_grad = summed[1].astype(jnp.bfloat16)
    value_weight_grad = lax.psum_scatter(
        jnp.einsum("sc,sk->ck", x_rows, value_grad, preferred_element_type=jnp.float32),
        ("dp", "ctx"),
        scatter_dimension=0,
        tiled=True,
    )
    return (query_grad, key_grad[None], value_grad[None], value_weight_grad)


def solution(mesh):
    placed = (
        P("dp", "ctx", None),
        P("dp", "ctx", None),
        P("dp", "ctx", None),
        P("dp", "ctx", None),
        P("dp", "ctx", None),
        P("dp", None),
    )
    return jax.shard_map(
        local,
        mesh=mesh,
        in_specs=placed,
        out_specs=(
            P("dp", "ctx", None),
            P("dp", "ctx", None),
            P("dp", "ctx", None),
            P(("dp", "ctx"), None),
        ),
        check_vma=False,
    )
```

profile of v0, /device:TPU:128, one launch (start us, length us, event | category | flops | bytes accessed | tf_op | source)
XLA Modules:
  0.0 1739.8 jit_solution(39723421712294179)
XLA Ops:
  7.2 2.0 constant_dynamic-update-slice_fusion.2
  9.2 1.9 constant_dynamic-update-slice_fusion.1
  11.1 5.1 collective-permute-start.1
  16.2 3.4 collective-permute-start
  20.5 4.1 copy.49
  24.6 4.1 copy.50
  28.8 16.2 collective-permute-done.1
  46.5 1.9 pad_maximum_fusion.2
  48.4 1.6 broadcast_in_dim.75.clone
  49.9 2.1 broadcast.40.clone
  52.0 2.0 broadcast.40
  54.0 110.6 %while.18 = (s32[]{:T(128)}, bf16[256,4096]{1,0:T(8,128)(2,1)}, f32[768,1024]{1,0:T(8,128)}, f32[768,1024]{1,0:T(8,128)}, bf16[768,1024]{1,0:T(8,128)(2,1)}, /*i...) while((s32[]{:T(128)}, bf16[256,4096]{1,0:T(8,128)(2,1)}, ...), condition=%wide.region_6.7_spmd.clone, body=%wide.region_2.6_spmd.clone.sunk | while | flops 1225816064 | bytes 33211708 | solution.py:86
  55.3 1.6 fusion.70
  57.6 1.8 fusion.72
  59.4 2.0 fusion.73
  61.4 1.5 fusion.75
  64.4 2.8 fusion.74
  69.2 1.6 fusion.70
  71.5 1.7 fusion.72
  73.2 2.0 fusion.73
  75.2 1.5 fusion.75
  76.7 1.3 convolution_multiply_fusion.2
  78.2 2.8 fusion.74
  83.0 1.6 fusion.70
  85.3 1.7 fusion.72
  87.0 2.0 fusion.73
  89.0 1.5 fusion.75
  90.6 1.3 convolution_multiply_fusion.2
  92.1 2.7 fusion.74
  96.8 1.6 fusion.70
  99.1 1.7 fusion.72
  100.8 2.0 fusion.73
  102.8 1.5 fusion.75
  105.8 2.8 fusion.74
  110.7 1.6 fusion.70
  112.9 1.8 fusion.72
  114.7 2.0 fusion.73
  116.7 1.5 fusion.75
  119.7 2.8 fusion.74
  124.5 1.6 fusion.70
  126.7 1.7 fusion.72
  128.5 2.0 fusion.73
  130.5 1.5 fusion.75
  133.5 2.8 fusion.74
  138.3 1.6 fusion.70
  140.6 1.7 fusion.72
  142.3 2.0 fusion.73
  144.3 1.5 fusion.75
  145.8 1.3 convolution_multiply_fusion.2
  147.3 2.8 fusion.74
  152.1 1.6 fusion.70
  154.4 1.7 fusion.72
  156.1 2.0 fusion.73
  158.1 1.5 fusion.75
  159.6 1.3 convolution_multiply_fusion.2
  161.1 2.8 fusion.74
  164.6 2.2 slice_bitcast_fusion.4
  168.0 1.9 collective-permute-start.3
  170.1 21.8 %collective-permute-start.2 = (f32[2,256,1024]{2,1,0:T(8,128)S(1)}, f32[2,256,1024]{2,1,0:T(8,128)S(1)}, u32[]{:S(2)}, u32[]{:S(2)}) collective-permute-start(f32[2,256,1024]{2,1,0:T(8,128)S(1)} %pad_maximum_fusion), channel_id=1, source_target_pairs={{1,0},{2,1},{3,2},{4,3},{5,4},{6,5},{7,6},{8,7},{9,8},{10,9},{11,1... | collective-permute-start | bytes 6291464 | tf_op jit(solution)/shard_map/ppermute | solution.py:15
  192.0 26.5 %collective-permute-done.3 = f32[2,256,1024]{2,1,0:T(8,128)S(1)} collective-permute-done((f32[2,256,1024]{2,1,0:T(8,128)S(1)}, f32[2,256,1024]{2,1,0:T(8,128)S(1)}, u32[]{:S(2)}, u32[]{:S(2)}) %collective-permute-start.3) | collective-permute-done | bytes 2097184 | tf_op jit(solution)/shard_map/ppermute | solution.py:15
  218.4 40.3 %collective-permute-done.2 = f32[2,256,1024]{2,1,0:T(8,128)S(1)} collective-permute-done((f32[2,256,1024]{2,1,0:T(8,128)S(1)}, f32[2,256,1024]{2,1,0:T(8,128)S(1)}, u32[]{:S(2)}, u32[]{:S(2)}) %collective-permute-start.2) | collective-permute-done | bytes 2097184 | tf_op jit(solution)/shard_map/ppermute | solution.py:15
  260.4 8.1 convolution_bitcast_fusion.3
  268.5 17.5 %copy.63 = f32[4096,1024]{1,0:T(8,128)} copy(f32[4096,1024]{0,1:T(8,128)} %convolution_bitcast_fusion.3) | data formatting | bytes 33554432
  286.0 1447.0 %reduce-scatter.4.cloned.1.call-done = f32[16,1024]{1,0:T(8,128)} async-done(((f32[4096,1024]{1,0:T(8,128)}), f32[16,1024]{1,0:T(8,128)}) %reduce-scatter.4.cloned.1.call-update) | async-done | bytes 65552
  (95 shorter events, 33.5 us)
Async XLA Ops:
  7.2 253.2 %copy-start = (bf16[1,256,4096]{2,1,0:T(8,128)(2,1)S(1)}, bf16[1,256,4096]{2,1,0:T(8,128)(2,1)}, u32[]{:S(2)}) copy-start(bf16[1,256,4096]{2,1,0:T(8,128)(2,1)} %param.12) | copy-start | bytes 6291460
  7.2 1725.8 %reduce-scatter.4.cloned.1.call-start = ((), (), s32[]{:S(2)}) async-start(), calls=%async_computation.1 | async-start | bytes 16842752
  11.1 34.0 %collective-permute-start.1 = (bf16[2,256,1024]{2,1,0:T(8,128)(2,1)}, bf16[2,256,1024]{2,1,0:T(8,128)(2,1)}, u32[]{:S(2)}, u32[]{:S(2)}) collective-permute-start(bf16[2,256,1024]{2,1,0:T(8,128)(2,1)} %constant_dynamic-update-slice_fusion.1), channel_id=1, source_target_pairs={{0,1},{1,2},{2,3},{3,4},{4,5},{5,6},{6,7},{7,8},{8,9},{9,10},{10,1... | collective-permute-start | bytes 3145736 | tf_op jit(solution)/shard_map/ppermute | solution.py:15
  16.2 30.1 %collective-permute-start = (bf16[2,256,1024]{2,1,0:T(8,128)(2,1)}, bf16[2,256,1024]{2,1,0:T(8,128)(2,1)S(1)}, u32[]{:S(2)}, u32[]{:S(2)}) collective-permute-start(bf16[2,256,1024]{2,1,0:T(8,128)(2,1)} %constant_dynamic-update-slice_fusion.1), channel_id=1, source_target_pairs={{0,2},{1,3},{2,4},{3,5},{4,6},{5,7},{6,8},{7,9},{8,10},{9,11},{10,... | collective-permute-start | bytes 3145736 | tf_op jit(solution)/shard_map/ppermute | solution.py:15
  24.6 4.1 copy-start.6
  28.7 17.7 %copy-start.4 = (bf16[1,256,1024]{2,1,0:T(8,128)(2,1)S(1)}, bf16[1,256,1024]{2,1,0:T(8,128)(2,1)}, u32[]{:S(2)}) copy-start(bf16[1,256,1024]{2,1,0:T(8,128)(2,1)} %param.9) | copy-start | bytes 1572868
  28.7 17.8 %copy-start.5 = (bf16[1,256,1024]{2,1,0:T(8,128)(2,1)S(1)}, bf16[1,256,1024]{2,1,0:T(8,128)(2,1)}, u32[]{:S(2)}) copy-start(bf16[1,256,1024]{2,1,0:T(8,128)(2,1)} %param.10) | copy-start | bytes 1572868
  61.4 2.9 copy-start.1
  75.2 2.9 copy-start.1
  89.0 2.9 copy-start.1
  102.8 2.9 copy-start.1
  116.7 2.9 copy-start.1
  130.5 2.9 copy-start.1
  144.3 2.8 copy-start.1
  158.1 2.8 copy-start.1
  164.6 2.8 copy-start.2
  168.0 50.5 %collective-permute-start.3 = (f32[2,256,1024]{2,1,0:T(8,128)S(1)}, f32[2,256,1024]{2,1,0:T(8,128)S(1)}, u32[]{:S(2)}, u32[]{:S(2)}) collective-permute-start(f32[2,256,1024]{2,1,0:T(8,128)S(1)} %pad_maximum_fusion.1), channel_id=1, source_target_pairs={{2,0},{3,1},{4,2},{5,3},{6,4},{7,5},{8,6},{9,7},{10,8},{11,9},{12,... | collective-permute-start | bytes 6291464 | tf_op jit(solution)/shard_map/ppermute | solution.py:15
  170.1 88.6 %collective-permute-start.2 = (f32[2,256,1024]{2,1,0:T(8,128)S(1)}, f32[2,256,1024]{2,1,0:T(8,128)S(1)}, u32[]{:S(2)}, u32[]{:S(2)}) collective-permute-start(f32[2,256,1024]{2,1,0:T(8,128)S(1)} %pad_maximum_fusion), channel_id=1, source_target_pairs={{1,0},{2,1},{3,2},{4,3},{5,4},{6,5},{7,6},{8,7},{9,8},{10,9},{11,1... | collective-permute-start | bytes 6291464 | tf_op jit(solution)/shard_map/ppermute | solution.py:15
  260.4 8.1 copy-start.3
Sparse Core Ops, SparseCore 0:
  286.1 1446.8 reduce-scatter.3
where the time goes:
time: 1740 us
  waiting for transfers between devices  1530 us (88%)
  matrix products  95.4 us (5%)
  local copies, waits for them, and re-layouts  56 us (3%)
  starting transfers between devices  32.3 us (2%)
    unnamed x2, waiting for transfers between devices  1450 us
    ppermute x4, waiting for transfers between devices, shifted(): return lax.ppermute(block, axis, route)  83.1 us
  transfers between devices with their start and end apart: 5, of which 4 were waited for; matrix products, arithmetic and copies ran while one was open for 1% of the time, Pallas kernels for 0%

commit v1 on v0

--- a/solution.py
+++ b/solution.py
@@ -1,6 +1,8 @@
 import jax
 import jax.numpy as jnp
 from jax import lax
+from jax.experimental import pallas as pl
+from jax.experimental.pallas import tpu as pltpu
 from jax.sharding import PartitionSpec as P
 
 KVH = 8
@@ -99,13 +101,195 @@
     query_grad = dq_acc.astype(jnp.bfloat16)[None]
     key_grad = summed[0].astype(jnp.bfloat16)
     value_grad = summed[1].astype(jnp.bfloat16)
-    value_weight_grad = lax.psum_scatter(
-        jnp.einsum("sc,sk->ck", x_rows, value_grad, preferred_element_type=jnp.float32),
-        ("dp", "ctx"),
-        scatter_dimension=0,
-        tiled=True,
-    )
+    value_weight_grad = weight_grad(x_rows, value_grad)
     return (query_grad, key_grad[None], value_grad[None], value_weight_grad)
+
+
+MESH = pl.DeviceIdType.MESH
+GROUPS = ((0, 256, "z"), (256, 256, "x"), (512, 256, "z"), (768, 256, "x"))
+
+
+def place():
+    dp, ctx = lax.axis_index("dp"), lax.axis_index("ctx")
+    return {
+        "core": lax.rem(dp, 2),
+        "y": lax.rem(ctx, 2) * 2 + dp // 2,
+        "x": lax.rem(ctx // 2, 4),
+        "z": ctx // 8,
+    }
+
+
+def at(here, axis=None, step=0):
+    spot = dict(here)
+    if axis is not None:
+        size = {"core": 2, "y": 4, "x": 4, "z": 8}[axis]
+        spot[axis] = lax.rem(spot[axis] + (step + size), size)
+    dp = lax.rem(spot["y"], 2) * 2 + spot["core"]
+    ctx = spot["z"] * 8 + spot["x"] * 2 + spot["y"] // 2
+    return (dp, ctx)
+
+
+def greet(targets):
+    barrier = pltpu.get_barrier_semaphore()
+    for target in targets:
+        pl.semaphore_signal(barrier, inc=1, device_id=target, device_id_type=MESH)
+    pl.semaphore_wait(barrier, len(targets))
+
+
+def push(src, dst, sems, slot, target):
+    copy = pltpu.make_async_remote_copy(
+        src_ref=src,
+        dst_ref=dst,
+        send_sem=sems.at[0, slot],
+        recv_sem=sems.at[1, slot],
+        device_id=target,
+        device_id_type=MESH,
+    )
+    copy.start()
+    return copy
+
+
+def ring(here, axis, term, keep, width, out, inn, sems, base):
+    size = {"x": 4, "z": 8}[axis]
+    half = size // 2
+    mid = width // 2
+    total_of = lambda step: lax.rem(here[axis] + step + size, size)
+    plus, minus = at(here, axis, 1), at(here, axis, -1)
+    copies = [[], []]
+    far = term(total_of(half)).astype(jnp.bfloat16)
+    out[0, 0, :, :mid] = far[:, :mid]
+    out[1, 0, :, mid:] = far[:, mid:]
+    copies[0].append(push(out.at[0, 0, :, pl.ds(0, mid)], inn.at[0, 0, :, pl.ds(0, mid)], sems, base, plus))
+    copies[1].append(push(out.at[1, 0, :, pl.ds(mid, mid)], inn.at[1, 0, :, pl.ds(mid, mid)], sems, base + 1, minus))
+    yield
+    for step in range(1, half):
+        for way, (sign, target) in enumerate(((1, plus), (-1, minus))):
+            mine = term(total_of(sign * (half - step)))
+            copies[way][-1].wait_recv()
+            if step == 1:
+                got = slice(0, mid) if way == 0 else slice(mid, width)
+                rest = slice(mid, width) if way == 0 else slice(0, mid)
+                out[way, step, :, got] = (mine[:, got] + inn[way, 0, :, got].astype(jnp.float32)).astype(jnp.bfloat16)
+                out[way, step, :, rest] = mine[:, rest].astype(jnp.bfloat16)
+            else:
+                out[way, step] = (mine + inn[way, step - 1].astype(jnp.float32)).astype(jnp.bfloat16)
+            copies[way].append(push(out.at[way, step], inn.at[way, step], sems, base + 2 * step + way, target))
+        yield
+    mine = term(here[axis])
+    copies[0][-1].wait_recv()
+    copies[1][-1].wait_recv()
+    keep(mine + inn[0, half - 1].astype(jnp.float32) + inn[1, half - 1].astype(jnp.float32))
+    for way in copies:
+        for copy in way:
+            copy.wait_send()
+    yield
+
+
+def scatter_group(here, xt, dvg, out_ref, c0, width, first, big_out, big_in, small_out, small_in, mid_sum, low_sum, y_out, y_in, sems):
+    def product(index):
+        if first == "z":
+            rows = xt[:, index].reshape(256, 512)
+        else:
+            rows = xt[:, :, index].reshape(512, 512)
+        return jnp.dot(rows, dvg[:, c0 : c0 + width], preferred_element_type=jnp.float32)
+
+    def keep_mid(value):
+        mid_sum[...] = value.reshape(mid_sum.shape)
+
+    def keep_low(value):
+        low_sum[...] = value.reshape(low_sum.shape)
+
+    second = "x" if first == "z" else "z"
+    yield from ring(here, first, product, keep_mid, width, big_out, big_in, sems, 0)
+    yield from ring(here, second, lambda index: mid_sum[:, index].reshape(64, width), keep_low, width, small_out, small_in, sems, 8)
+    copies = []
+    for step in range(1, 4):
+        target = lax.rem(here["y"] + step, 4)
+        y_out[step - 1] = low_sum[lax.rem(target, 2), target // 2].astype(jnp.bfloat16)
+        copies.append(push(y_out.at[step - 1], y_in.at[step - 1], sems, 16 + step, at(here, "y", step)))
+    yield
+    value = low_sum[lax.rem(here["y"], 2), here["y"] // 2]
+    for step in range(1, 4):
+        copies[step - 1].wait_recv()
+        value = value + y_in[step - 1].astype(jnp.float32)
+    out_ref[:, c0 : c0 + width] = value
+    for copy in copies:
+        copy.wait_send()
+
+
+def weight_kernel(x_ref, dv_ref, out_ref, xrecv, dvg, xt, pair_sems, *scratch):
+    here = place()
+    greet([at(here, "core", 1), at(here, "z", 1), at(here, "z", -1), at(here, "x", 1), at(here, "x", -1),
+           at(here, "y", 1), at(here, "y", 2), at(here, "y", 3)])
+    partner = at(here, "core", 1)
+    mine, other = here["core"] * 1024, (1 - here["core"]) * 1024
+    swaps = [push(dv_ref, dvg.at[pl.ds(256, 256)], pair_sems, 2, partner)]
+    for part in range(2):
+        columns = pl.ds(pl.multiple_of(part * 2048 + other, 128), 1024)
+        swaps.append(push(x_ref.at[:, columns], xrecv.at[:, pl.ds(part * 1024, 1024)], pair_sems, part, partner))
+    dvg[0:256] = dv_ref[...]
+    for part in range(2):
+        def own(z, carry):
+            columns = pl.ds(pl.multiple_of(part * 2048 + mine + z * 128, 128), 128)
+            xt[part, z, :, :, 0:256] = x_ref[:, columns].T.reshape(4, 32, 256)
+            return carry
+        lax.fori_loop(0, 8, own, 0)
+    for swap in swaps:
+        swap.wait()
+    for part in range(2):
+        def got(z, carry):
+            columns = pl.ds(pl.multiple_of(part * 1024 + z * 128, 128), 128)
+            xt[part, z, :, :, 256:512] = xrecv[:, columns].T.reshape(4, 32, 256)
+            return carry
+        lax.fori_loop(0, 8, got, 0)
+    per = len(scratch) // len(GROUPS)
+    running = [
+        scatter_group(here, xt, dvg, out_ref, c0, width, first, *scratch[i * per : (i + 1) * per])
+        for i, (c0, width, first) in enumerate(GROUPS)
+    ]
+    while running:
+        alive = []
+        for group in running:
+            if next(group, "end") != "end":
+                alive.append(group)
+        running = alive
+
+
+def group_scratch(width, first):
+    big, small, span = ((4, 256), (2, 64), (2, 4, 32)) if first == "z" else ((2, 512), (4, 64), (2, 8, 32))
+    return [
+        pltpu.VMEM((2, *big, width), jnp.bfloat16),
+        pltpu.VMEM((2, *big, width), jnp.bfloat16),
+        pltpu.VMEM((2, *small, width), jnp.bfloat16),
+        pltpu.VMEM((2, *small, width), jnp.bfloat16),
+        pltpu.VMEM((*span, width), jnp.float32),
+        pltpu.VMEM((2, 2, 16, width), jnp.float32),
+        pltpu.VMEM((3, 16, width), jnp.bfloat16),
+        pltpu.VMEM((3, 16, width), jnp.bfloat16),
+        pltpu.SemaphoreType.DMA((2, 20)),
+    ]
+
+
+def weight_grad(x_rows, dv_rows):
+    scratch = [
+        pltpu.VMEM((256, 2048), jnp.bfloat16),
+        pltpu.VMEM((512, 1024), jnp.bfloat16),
+        pltpu.VMEM((2, 8, 4, 32, 512), jnp.bfloat16),
+        pltpu.SemaphoreType.DMA((2, 3)),
+    ]
+    for _, width, first in GROUPS:
+        scratch += group_scratch(width, first)
+    return pl.pallas_call(
+        weight_kernel,
+        out_shape=jax.ShapeDtypeStruct((16, 1024), jnp.float32),
+        in_specs=[pl.BlockSpec(memory_space=pltpu.VMEM)] * 2,
+        out_specs=pl.BlockSpec(memory_space=pltpu.VMEM),
+        scratch_shapes=scratch,
+        compiler_params=pltpu.CompilerParams(
+            collective_id=1, has_side_effects=True, vmem_limit_bytes=48 * 2**20
+        ),
+        cost_estimate=pl.CostEstimate(flops=2 * 256 * 4096 * 1024, bytes_accessed=8 * 2**20, transcendentals=0),
+    )(x_rows, dv_rows)
 
 
 def solution(mesh):

time: 1740 us -> 309 us (0.18)
  the two profiles are of different devices: /device:TPU:128 before, /device:TPU:32 now
where the time goes in v1:
time: 309 us; the launch traced here: 308 us
  waiting for transfers between devices  124 us (40%)
  matrix products  61.5 us (20%)
  Pallas kernels  59.2 us (19%)
  local copies, waits for them, and re-layouts  38.6 us (12%)
  starting transfers between devices  12.7 us (4%)
  other arithmetic  10.9 us (4%)
    ppermute x4, waiting for transfers between devices, shifted(): return lax.ppermute(block, axis, route)  124 us
    pallas_call x1, Pallas kernels, weight_grad(): pl.pallas_call(weight_kernel, out_shape=jax.ShapeDtypeStruct((16, 1024),...  59.2 us
    dot_general x8, matrix products, group_grads(): jnp.einsum('sed,wd->esw', do_group, v_group, preferred_element_type=jnp.f...  15.9 us
    dot_general x8, matrix products, group_grads(): jnp.einsum('esw,wd->sed', probs_b, v_group, preferred_element_type=jnp.fl...  13.9 us
    ppermute x4, starting transfers between devices, shifted(): return lax.ppermute(block, axis, route)  12.7 us
    dot_general x8, matrix products, group_grads(): jnp.einsum('esw,sed->wd', probs_b, do_group, preferred_element_type=jnp.f...  12.1 us
    dot_general x8, matrix products, group_grads(): jnp.einsum('esw,sed->wd', dscores_b, q_group, preferred_element_type=jnp....  11 us
    unnamed x16, local copies, waits for them, and re-layouts  9.22 us
  transfers between devices with their start and end apart: 4, of which 4 were waited for; matrix products, arithmetic and copies ran while one was open for 3% of the time, Pallas kernels for 0%

profile of v1, /device:TPU:32, one launch (start us, length us, event | category | flops | bytes accessed | tf_op | source)
XLA Modules:
  0.0 307.6 jit_solution(7756044197238871335)
XLA Ops:
  0.6 2.0 constant_dynamic-update-slice_fusion.2
  2.7 1.9 constant_dynamic-update-slice_fusion.1
  4.5 3.4 %collective-permute-start = (bf16[2,256,1024]{2,1,0:T(8,128)(2,1)}, bf16[2,256,1024]{2,1,0:T(8,128)(2,1)}, u32[]{:S(2)}, u32[]{:S(2)}) collective-permute-start(bf16[2,256,1024]{2,1,0:T(8,128)(2,1)} %constant_dynamic-update-slice_fusion.1), channel_id=1, source_target_pairs={{0,2},{1,3},{2,4},{3,5},{4,6},{5,7},{6,8},{7,9},{8,10},{9,11},{10,... | collective-permute-start | bytes 3145736 | tf_op jit(solution)/shard_map/ppermute | solution.py:17
  7.9 5.1 %collective-permute-start.1 = (bf16[2,256,1024]{2,1,0:T(8,128)(2,1)}, bf16[2,256,1024]{2,1,0:T(8,128)(2,1)S(1)}, u32[]{:S(2)}, u32[]{:S(2)}) collective-permute-start(bf16[2,256,1024]{2,1,0:T(8,128)(2,1)} %constant_dynamic-update-slice_fusion.1), channel_id=1, source_target_pairs={{0,1},{1,2},{2,3},{3,4},{4,5},{5,6},{6,7},{7,8},{8,9},{9,10},{10,1... | collective-permute-start | bytes 3145736 | tf_op jit(solution)/shard_map/ppermute | solution.py:17
  13.0 0.9 reduce-window_clone.1
  13.9 2.5 copy.35
  16.4 4.1 %copy.36 = bf16[1,256,4096]{1,2,0:T(8,128)(2,1)} copy(bf16[1,256,4096]{2,1,0:T(8,128)(2,1)} %param.11) | data formatting | bytes 4194304 | tf_op args[3]
  20.6 13.1 %collective-permute-done = bf16[2,256,1024]{2,1,0:T(8,128)(2,1)} collective-permute-done((bf16[2,256,1024]{2,1,0:T(8,128)(2,1)}, bf16[2,256,1024]{2,1,0:T(8,128)(2,1)}, u32[]{:S(2)}, u32[]{:S(2)}) %collective-permute-start) | collective-permute-done | bytes 1048608 | tf_op jit(solution)/shard_map/ppermute | solution.py:17
  33.7 1.3 slice_bitcast_fusion.7
  35.0 23.7 %collective-permute-done.1 = bf16[2,256,1024]{2,1,0:T(8,128)(2,1)S(1)} collective-permute-done((bf16[2,256,1024]{2,1,0:T(8,128)(2,1)}, bf16[2,256,1024]{2,1,0:T(8,128)(2,1)S(1)}, u32[]{:S(2)}, u32[]{:S(2)}) %collective-permute-start.1) | collective-permute-done | bytes 1048608 | tf_op jit(solution)/shard_map/ppermute | solution.py:17
  58.8 1.4 pad_maximum_fusion.2
  60.2 2.0 broadcast.40
  62.2 2.1 broadcast.40.clone
  64.3 1.6 broadcast_in_dim.75.clone
  65.8 84.7 %while.18 = (s32[]{:T(128)}, bf16[256,4096]{1,0:T(8,128)(2,1)}, f32[768,1024]{1,0:T(8,128)}, f32[768,1024]{1,0:T(8,128)}, bf16[768,1024]{1,0:T(8,128)(2,1)S(1)},...) while((s32[]{:T(128)}, bf16[256,4096]{1,0:T(8,128)(2,1)}, ...), condition=%wide.region_6.7_spmd.clone, body=%wide.region_2.6_spmd.clone.sunk | while | flops 1225816064 | bytes 26920216 | solution.py:88
  65.8 1.1 constant_dynamic-slice_fusion.3
  68.5 1.5 fusion.72
  70.0 1.7 fusion.69
  71.8 2.0 fusion.70
  73.8 1.4 fusion.71
  76.4 1.1 constant_dynamic-slice_fusion.3
  79.1 1.5 fusion.72
  80.6 1.7 fusion.69
  82.4 2.0 fusion.70
  84.4 1.4 fusion.71
  87.0 1.1 constant_dynamic-slice_fusion.3
  89.7 1.5 fusion.72
  91.2 1.7 fusion.69
  92.9 2.0 fusion.70
  94.9 1.4 fusion.71
  97.6 1.1 constant_dynamic-slice_fusion.3
  100.3 1.5 fusion.72
  101.8 1.7 fusion.69
  103.5 2.0 fusion.70
  105.5 1.4 fusion.71
  108.2 1.1 constant_dynamic-slice_fusion.3
  110.8 1.5 fusion.72
  112.3 1.7 fusion.69
  114.1 2.0 fusion.70
  116.1 1.4 fusion.71
  118.8 1.1 constant_dynamic-slice_fusion.3
  121.4 1.5 fusion.72
  123.0 1.7 fusion.69
  124.7 2.0 fusion.70
  126.7 1.4 fusion.71
  129.4 1.1 constant_dynamic-slice_fusion.3
  132.0 1.5 fusion.72
  133.5 1.7 fusion.69
  135.3 2.0 fusion.70
  137.3 1.3 fusion.71
  139.9 1.1 constant_dynamic-slice_fusion.3
  142.6 1.5 fusion.72
  144.1 1.7 fusion.69
  145.8 2.0 fusion.70
  147.8 1.4 fusion.71
  150.5 2.1 slice_bitcast_fusion.5
  152.6 2.1 slice_bitcast_fusion.4
  154.9 1.9 collective-permute-start.2
  157.1 2.3 collective-permute-start.3
  159.4 45.4 %collective-permute-done.2 = f32[2,256,1024]{2,1,0:T(8,128)S(1)} collective-permute-done((f32[2,256,1024]{2,1,0:T(8,128)S(1)}, f32[2,256,1024]{2,1,0:T(8,128)S(1)}, u32[]{:S(2)}, u32[]{:S(2)}) %collective-permute-start.2) | collective-permute-done | bytes 2097184 | tf_op jit(solution)/shard_map/ppermute | solution.py:17
  204.8 41.2 %collective-permute-done.3 = f32[2,256,1024]{2,1,0:T(8,128)S(1)} collective-permute-done((f32[2,256,1024]{2,1,0:T(8,128)S(1)}, f32[2,256,1024]{2,1,0:T(8,128)S(1)}, u32[]{:S(2)}, u32[]{:S(2)}) %collective-permute-start.3) | collective-permute-done | bytes 2097184 | tf_op jit(solution)/shard_map/ppermute | solution.py:17
  246.1 0.8 fusion.31
  246.9 0.9 fusion.32
  247.7 59.2 %shard_map.93 = f32[16,1024]{1,0:T(8,128)S(1)} custom-call(bf16[256,4096]{1,0:T(8,128)(2,1)S(1)} %bitcast.148, bf16[256,1024]{1,0:T(8,128)(2,1)S(1)} %bitcast.147), custom_call_target="tpu_custom_call" | custom-call | flops 2147483648 | bytes 8388608 | tf_op jit(solution)/shard_map/pallas_call | solution.py:282
  (76 shorter events, 24.1 us)
Async XLA Ops:
  0.6 13.3 %copy-start.4 = (bf16[1,256,4096]{2,1,0:T(8,128)(2,1)S(1)}, bf16[1,256,4096]{2,1,0:T(8,128)(2,1)}, u32[]{:S(2)}) copy-start(bf16[1,256,4096]{2,1,0:T(8,128)(2,1)} %param.8) | copy-start | bytes 6291460
  4.5 29.2 %collective-permute-start = (bf16[2,256,1024]{2,1,0:T(8,128)(2,1)}, bf16[2,256,1024]{2,1,0:T(8,128)(2,1)}, u32[]{:S(2)}, u32[]{:S(2)}) collective-permute-start(bf16[2,256,1024]{2,1,0:T(8,128)(2,1)} %constant_dynamic-update-slice_fusion.1), channel_id=1, source_target_pairs={{0,2},{1,3},{2,4},{3,5},{4,6},{5,7},{6,8},{7,9},{8,10},{9,11},{10,... | collective-permute-start | bytes 3145736 | tf_op jit(solution)/shard_map/ppermute | solution.py:17
  7.9 50.8 %collective-permute-start.1 = (bf16[2,256,1024]{2,1,0:T(8,128)(2,1)}, bf16[2,256,1024]{2,1,0:T(8,128)(2,1)S(1)}, u32[]{:S(2)}, u32[]{:S(2)}) collective-permute-start(bf16[2,256,1024]{2,1,0:T(8,128)(2,1)} %constant_dynamic-update-slice_fusion.1), channel_id=1, source_target_pairs={{0,1},{1,2},{2,3},{3,4},{4,5},{5,6},{6,7},{7,8},{8,9},{9,10},{10,1... | collective-permute-start | bytes 3145736 | tf_op jit(solution)/shard_map/ppermute | solution.py:17
  16.4 4.1 %copy-start.5 = (s32[1,64]{1,0:T(1,128)S(1)}, s32[1,64]{1,0:T(1,128)}, u32[]{:S(2)}) copy-start(s32[1,64]{1,0:T(1,128)} %param.13) | copy-start | bytes 772
  20.5 38.3 %copy-start.2 = (bf16[1,256,1024]{2,1,0:T(8,128)(2,1)S(1)}, bf16[1,256,1024]{2,1,0:T(8,128)(2,1)}, u32[]{:S(2)}) copy-start(bf16[1,256,1024]{2,1,0:T(8,128)(2,1)} %param.9) | copy-start | bytes 1572868
  20.5 38.3 %copy-start.3 = (bf16[1,256,1024]{2,1,0:T(8,128)(2,1)S(1)}, bf16[1,256,1024]{2,1,0:T(8,128)(2,1)}, u32[]{:S(2)}) copy-start(bf16[1,256,1024]{2,1,0:T(8,128)(2,1)} %param.10) | copy-start | bytes 1572868
  154.9 49.9 %collective-permute-start.2 = (f32[2,256,1024]{2,1,0:T(8,128)S(1)}, f32[2,256,1024]{2,1,0:T(8,128)S(1)}, u32[]{:S(2)}, u32[]{:S(2)}) collective-permute-start(f32[2,256,1024]{2,1,0:T(8,128)S(1)} %pad_maximum_fusion), channel_id=1, source_target_pairs={{1,0},{2,1},{3,2},{4,3},{5,4},{6,5},{7,6},{8,7},{9,8},{10,9},{11,1... | collective-permute-start | bytes 6291464 | tf_op jit(solution)/shard_map/ppermute | solution.py:17
  157.1 89.0 %collective-permute-start.3 = (f32[2,256,1024]{2,1,0:T(8,128)S(1)}, f32[2,256,1024]{2,1,0:T(8,128)S(1)}, u32[]{:S(2)}, u32[]{:S(2)}) collective-permute-start(f32[2,256,1024]{2,1,0:T(8,128)S(1)} %pad_maximum_fusion.1), channel_id=1, source_target_pairs={{2,0},{3,1},{4,2},{5,3},{6,4},{7,5},{8,6},{9,7},{10,8},{11,9},{12,... | collective-permute-start | bytes 6291464 | tf_op jit(solution)/shard_map/ppermute | solution.py:17
  246.1 1.7 copy-start.1
  247.7 59.2 %copy-start = (bf16[1,256,1024]{2,1,0:T(8,128)(2,1)}, bf16[1,256,1024]{2,1,0:T(8,128)(2,1)S(1)}, u32[]{:S(2)}) copy-start(bf16[1,256,1024]{2,1,0:T(8,128)(2,1)S(1)} %get-tuple-element.362) | copy-start | bytes 1572868

commit v2 on v1

v2 whole, which is shorter than its diff:
```python
import jax
import jax.numpy as jnp
from jax import lax
from jax.experimental import pallas as pl
from jax.experimental.pallas import tpu as pltpu
from jax.sharding import PartitionSpec as P

KVH = 8
HD = 128
GROUP = 4
RS_FROM = 20
RS_EVERY = 0
MESH = pl.DeviceIdType.MESH
GROUPS = ((0, 256, "z"), (256, 256, "x"), (512, 256, "z"), (768, 256, "x"))


def place():
    dp, ctx = lax.axis_index("dp"), lax.axis_index("ctx")
    return {
        "core": lax.rem(dp, 2),
        "y": lax.rem(ctx, 2) * 2 + dp // 2,
        "x": lax.rem(ctx // 2, 4),
        "z": ctx // 8,
    }


def at(here, axis=None, step=0):
    spot = dict(here)
    if axis is not None:
        size = {"core": 2, "y": 4, "x": 4, "z": 8}[axis]
        spot[axis] = lax.rem(spot[axis] + (step + size), size)
    dp = lax.rem(spot["y"], 2) * 2 + spot["core"]
    ctx = spot["z"] * 8 + spot["x"] * 2 + spot["y"] // 2
    return (dp, ctx)


def greet(targets):
    barrier = pltpu.get_barrier_semaphore()
    for target in targets:
        pl.semaphore_signal(barrier, inc=1, device_id=target, device_id_type=MESH)
    pl.semaphore_wait(barrier, len(targets))


def push(src, dst, sems, slot, target):
    copy = pltpu.make_async_remote_copy(
        src_ref=src,
        dst_ref=dst,
        send_sem=sems.at[0, slot],
        recv_sem=sems.at[1, slot],
        device_id=target,
        device_id_type=MESH,
    )
    copy.start()
    return copy


def ring(here, axis, term, keep, width, out, inn, sems, base):
    size = {"x": 4, "z": 8}[axis]
    half = size // 2
    mid = width // 2
    total_of = lambda step: lax.rem(here[axis] + step + size, size)
    plus, minus = at(here, axis, 1), at(here, axis, -1)
    copies = [[], []]
    far = term(total_of(half)).astype(jnp.bfloat16)
    out[0, 0, :, :mid] = far[:, :mid]
    out[1, 0, :, mid:] = far[:, mid:]
    copies[0].append(push(out.at[0, 0, :, pl.ds(0, mid)], inn.at[0, 0, :, pl.ds(0, mid)], sems, base, plus))
    copies[1].append(push(out.at[1, 0, :, pl.ds(mid, mid)], inn.at[1, 0, :, pl.ds(mid, mid)], sems, base + 1, minus))
    yield
    for step in range(1, half):
        for way, (sign, target) in enumerate(((1, plus), (-1, minus))):
            mine = term(total_of(sign * (half - step)))
            copies[way][-1].wait_recv()
            if step == 1:
                got = slice(0, mid) if way == 0 else slice(mid, width)
                rest = slice(mid, width) if way == 0 else slice(0, mid)
                out[way, step, :, got] = (mine[:, got] + inn[way, 0, :, got].astype(jnp.float32)).astype(jnp.bfloat16)
                out[way, step, :, rest] = mine[:, rest].astype(jnp.bfloat16)
            else:
                out[way, step] = (mine + inn[way, step - 1].astype(jnp.float32)).astype(jnp.bfloat16)
            copies[way].append(push(out.at[way, step], inn.at[way, step], sems, base + 2 * step + way, target))
        yield
    mine = term(here[axis])
    copies[0][-1].wait_recv()
    copies[1][-1].wait_recv()
    keep(mine + inn[0, half - 1].astype(jnp.float32) + inn[1, half - 1].astype(jnp.float32))
    for way in copies:
        for copy in way:
            copy.wait_send()
    yield


def scatter_group(here, xt, dvg, out_ref, c0, width, first, big_out, big_in, small_out, small_in, mid_sum, low_sum, y_out, y_in, sems):
    def product(index):
        if first == "z":
            rows = xt[:, index].reshape(256, 512)
        else:
            rows = xt[:, :, index].reshape(512, 512)
        return jnp.dot(rows, dvg[:, c0 : c0 + width], preferred_element_type=jnp.float32)

    def keep_mid(value):
        mid_sum[...] = value.reshape(mid_sum.shape)

    def keep_low(value):
        low_sum[...] = value.reshape(low_sum.shape)

    second = "x" if first == "z" else "z"
    yield from ring(here, first, product, keep_mid, width, big_out, big_in, sems, 0)
    yield from ring(here, second, lambda index: mid_sum[:, index].reshape(64, width), keep_low, width, small_out, small_in, sems, 8)
    copies = []
    for step in range(1, 4):
        target = lax.rem(here["y"] + step, 4)
        y_out[step - 1] = low_sum[lax.rem(target, 2), target // 2].astype(jnp.bfloat16)
        copies.append(push(y_out.at[step - 1], y_in.at[step - 1], sems, 16 + step, at(here, "y", step)))
    yield
    value = low_sum[lax.rem(here["y"], 2), here["y"] // 2]
    for step in range(1, 4):
        copies[step - 1].wait_recv()
        value = value + y_in[step - 1].astype(jnp.float32)
    out_ref[:, c0 : c0 + width] = value
    for copy in copies:
        copy.wait_send()


def group_scratch(width, first):
    big, small, span = ((4, 256), (2, 64), (2, 4, 32)) if first == "z" else ((2, 512), (4, 64), (2, 8, 32))
    return [
        pltpu.VMEM((2, *big, width), jnp.bfloat16),
        pltpu.VMEM((2, *big, width), jnp.bfloat16),
        pltpu.VMEM((2, *small, width), jnp.bfloat16),
        pltpu.VMEM((2, *small, width), jnp.bfloat16),
        pltpu.VMEM((*span, width), jnp.float32),
        pltpu.VMEM((2, 2, 16, width), jnp.float32),
        pltpu.VMEM((3, 16, width), jnp.bfloat16),
        pltpu.VMEM((3, 16, width), jnp.bfloat16),
        pltpu.SemaphoreType.DMA((2, 20)),
    ]


SPAN = 640
HALF = 128
SCALE = HD ** (-0.5)
BF = jnp.bfloat16
F32 = jnp.float32


def dot_nt(left, right):
    return lax.dot_general(left, right, (((1,), (1,)), ((), ())), preferred_element_type=F32)


def dot_nn(left, right):
    return jnp.dot(left, right, preferred_element_type=F32)


def head_columns(head, count=1):
    return pl.ds(pl.multiple_of(head * HD, HD), count * HD)


def stacked(ref, g, half):
    rows = pl.ds(half * HALF, HALF)
    return jnp.concatenate([ref[rows, head_columns(g * GROUP + e)] for e in range(GROUP)], axis=0)


def fill_bias(lengths_ref, slab, bias):
    row = lax.broadcasted_iota(jnp.int32, (64, 64), 0)
    col = lax.broadcasted_iota(jnp.int32, (64, 64), 1)
    sizes = jnp.broadcast_to(lengths_ref[...], (64, 64))
    starts = jnp.sum(jnp.where(col < row, sizes, 0), axis=1, keepdims=True)
    for half in range(2):
        base = slab * 256 + half * HALF
        query = base + lax.broadcasted_iota(jnp.int32, (64, HALF), 1)
        first = jnp.max(jnp.where(starts <= query, starts, 0), axis=0, keepdims=True)
        key = base - 512 + lax.broadcasted_iota(jnp.int32, (SPAN, HALF), 0)
        query = base + lax.broadcasted_iota(jnp.int32, (SPAN, HALF), 1)
        value = jnp.where((key <= query) & (key >= first), 0.0, -1e30)
        for e in range(GROUP):
            bias[half, :, e * HALF : (e + 1) * HALF] = value


def probs_step(g, q_ref, do_ref, kwin, bias, pbuf, dvwin):
    for half in range(2):
        rows = pl.ds(half * HALF, SPAN)
        scores = dot_nt(kwin[g, rows], stacked(q_ref, g, half)) * (SCALE * 1.4426950408889634) + bias[half]
        top = jnp.max(scores, axis=0, keepdims=True)
        weights = jnp.exp2(scores - top)
        probs = (weights * (1.0 / jnp.sum(weights, axis=0, keepdims=True))).astype(BF)
        pbuf[g, half] = probs
        term = dot_nn(probs, stacked(do_ref, g, half))
        if half == 0:
            dvwin[0:SPAN] = term
            dvwin[SPAN:768] = jnp.zeros((HALF, HD), F32)
        else:
            dvwin[rows] += term


def grads_step(g, q_ref, do_ref, kwin, vwin, pbuf, dkwin, dq_ref):
    turned = kwin[g].T
    for half in range(2):
        rows = pl.ds(half * HALF, SPAN)
        probs = pbuf[g, half].astype(F32)
        dprobs = dot_nt(vwin[g, rows], stacked(do_ref, g, half))
        delta = jnp.sum(probs * dprobs, axis=0, keepdims=True)
        dscores = (probs * (dprobs - delta)).astype(BF)
        term = dot_nn(dscores, stacked(q_ref, g, half))
        if half == 0:
            dkwin[0:SPAN] = term
            dkwin[SPAN:768] = jnp.zeros((HALF, HD), F32)
        else:
            dkwin[rows] += term
        dq = dot_nn(turned[:, half * HALF : half * HALF + SPAN], dscores) * SCALE
        for e in range(GROUP):
            dq_ref[pl.ds(half * HALF, HALF), head_columns(g * GROUP + e)] = dq[:, e * HALF : (e + 1) * HALF].T.astype(BF)


LEAD = 3


def fused_kernel(lengths_ref, q_ref, k_ref, v_ref, do_ref, x_ref, dq_ref, dk_ref, dv_ref, dw_ref,
                 kwin, vwin, bias, pbuf, window, out1, in1, out2, in2, final, xrecv, dvg, xt, halo_sems, pair_sems, *scratch):
    here = place()
    dp, ctx = lax.axis_index("dp"), lax.axis_index("ctx")
    odd = lax.rem(ctx, 2)
    twin = (dp, ctx + 1 - 2 * odd)
    ahead, behind = (dp, lax.rem(ctx + 2, 64)), (dp, lax.rem(ctx + 62, 64))
    partner = at(here, "core", 1)
    relay = pl.multiple_of(512 * (1 - odd), 256)

    def link(src, dst, kind, g, target):
        return pltpu.make_async_remote_copy(
            src_ref=src, dst_ref=dst, send_sem=halo_sems.at[0, kind, g], recv_sem=halo_sems.at[1, kind, g],
            device_id=target, device_id_type=MESH)

    def halo_x(which, g):
        win = (kwin, vwin)[which]
        return link(win.at[g, pl.ds(512, 256)], win.at[g, pl.ds(0, 256)], 2 * which, g, ahead)

    def halo_y(which, g):
        win = (kwin, vwin)[which]
        return link(win.at[g, pl.ds(relay, 256)], win.at[g, pl.ds(256, 256)], 2 * which + 1, g, twin)

    def back_y(which, g):
        return link(out1.at[which, g], in1.at[which, g], 4 + 2 * which, g, twin)

    def back_x(which, g):
        return link(out2.at[which, g], in2.at[which, g], 5 + 2 * which, g, behind)

    def forward(which, g):
        halo_x(which, g).wait_recv()
        halo_y(which, g).start()

    def give_near(which, g):
        out1[which, g] = window[256:512].astype(BF)
        final[which, g] = window[512:768]
        out2[which, g] = window[0:256].astype(BF)
        back_y(which, g).start()

    def give_far(which, g):
        back_y(which, g).wait_recv()
        got = in1[which, g].astype(F32)
        out2[which, g] = (out2[which, g].astype(F32) + jnp.where(odd == 1, got, 0.0)).astype(BF)
        final[which, g] += jnp.where(odd == 1, 0.0, got)
        back_x(which, g).start()

    def finish(which, g):
        back_x(which, g).wait_recv()
        total = final[which, g] + in2[which, g].astype(F32)
        if which == 0:
            dk_ref[:, head_columns(g)] = (total * SCALE).astype(BF)
        else:
            rounded = total.astype(BF)
            dv_ref[:, head_columns(g)] = rounded
            dvg[0:256, head_columns(g)] = rounded

    swaps = []

    def share(g):
        columns = pl.ds(g * HD, 2 * HD)
        swaps.append(push(dvg.at[pl.ds(0, 256), columns], dvg.at[pl.ds(256, 256), columns], pair_sems, 2 + g // 2, partner))

    for g in range(KVH):
        kwin[g, 512:768] = k_ref[:, g * HD : (g + 1) * HD]
        vwin[g, 512:768] = v_ref[:, g * HD : (g + 1) * HD]
    greet([partner, at(here, "z", 1), at(here, "z", -1), at(here, "x", 1), at(here, "x", -1),
           at(here, "y", 1), at(here, "y", 2), at(here, "y", 3), ahead, behind])
    for which in range(2):
        for g in range(KVH):
            halo_x(which, g).start()
    mine, other = here["core"] * 1024, (1 - here["core"]) * 1024
    for part in range(2):
        columns = pl.ds(pl.multiple_of(part * 2048 + other, 128), 1024)
        swaps.append(push(x_ref.at[:, columns], xrecv.at[:, pl.ds(part * 1024, 1024)], pair_sems, part, partner))
    fill_bias(lengths_ref, ctx, bias)
    for g in range(LEAD):
        forward(0, g)
    for part in range(2):
        def own(z, carry):
            columns = pl.ds(pl.multiple_of(part * 2048 + mine + z * 128, 128), 128)
            xt[part, z, :, :, 0:256] = x_ref[:, columns].T.reshape(4, 32, 256)
            return carry
        lax.fori_loop(0, 8, own, 0)

    def tail(which, tick):
        if 0 <= tick - 2 < KVH:
            give_far(which, tick - 2)
        if 0 <= tick - 4 < KVH:
            finish(which, tick - 4)
            if which == 1 and (tick - 4) % 2 == 1:
                share(tick - 5)

    groups = []
    values_late = {5: (0,), 6: (1, 2), 7: (3, 4), 8: (5, 6), 9: (7,)}
    per = len(scratch) // len(GROUPS)
    for tick in range(2 * KVH + 5):
        for g in values_late.get(tick, ()):
            forward(1, g)
        if tick + LEAD < KVH:
            forward(0, tick + LEAD)
        if tick < KVH:
            halo_y(0, tick).wait_recv()
            probs_step(tick, q_ref, do_ref, kwin, bias, pbuf, window)
            give_near(1, tick)
        elif tick < 2 * KVH:
            halo_y(1, tick - KVH).wait_recv()
            grads_step(tick - KVH, q_ref, do_ref, kwin, vwin, pbuf, window, dq_ref)
            give_near(0, tick - KVH)
        tail(1, tick)
        tail(0, tick - KVH)
        if tick == 7:
            swaps[0].wait()
            swaps[1].wait()
            for part in range(2):
                def got(z, carry):
                    columns = pl.ds(pl.multiple_of(part * 1024 + z * 128, 128), 128)
                    xt[part, z, :, :, 256:512] = xrecv[:, columns].T.reshape(4, 32, 256)
                    return carry
                lax.fori_loop(0, 8, got, 0)
        for i, (c0, width, first) in enumerate(GROUPS):
            if tick == RS_FROM + RS_EVERY * i:
                swaps[2 + i].wait()
                groups.append(scatter_group(here, xt, dvg, dw_ref, c0, width, first, *scratch[i * per : (i + 1) * per]))
        groups = [group for group in groups if next(group, "end") != "end"]
    while groups:
        groups = [group for group in groups if next(group, "end") != "end"]
    for which in range(2):
        for g in range(KVH):
            halo_x(which, g).wait_send()
            halo_y(which, g).wait_send()
            back_y(which, g).wait_send()
            back_x(which, g).wait_send()


def fused(lengths, q_rows, k_rows, v_rows, do_rows, x_rows):
    scratch = [
        pltpu.VMEM((KVH, 768, HD), BF),
        pltpu.VMEM((KVH, 768, HD), BF),
        pltpu.VMEM((2, SPAN, GROUP * HALF), F32),
        pltpu.VMEM((KVH, 2, SPAN, GROUP * HALF), BF),
        pltpu.VMEM((768, HD), F32),
        pltpu.VMEM((2, KVH, 256, HD), BF),
        pltpu.VMEM((2, KVH, 256, HD), BF),
        pltpu.VMEM((2, KVH, 256, HD), BF),
        pltpu.VMEM((2, KVH, 256, HD), BF),
        pltpu.VMEM((2, KVH, 256, HD), F32),
        pltpu.VMEM((256, 2048), BF),
        pltpu.VMEM((512, 1024), BF),
        pltpu.VMEM((2, 8, 4, 32, 512), BF),
        pltpu.SemaphoreType.DMA((2, 8, KVH)),
        pltpu.SemaphoreType.DMA((2, 6)),
    ]
    for _, width, first in GROUPS:
        scratch += group_scratch(width, first)
    return pl.pallas_call(
        fused_kernel,
        out_shape=(
            jax.ShapeDtypeStruct((256, 4096), BF),
            jax.ShapeDtypeStruct((256, 1024), BF),
            jax.ShapeDtypeStruct((256, 1024), BF),
            jax.ShapeDtypeStruct((16, 1024), F32),
        ),
        in_specs=[pl.BlockSpec(memory_space=pltpu.VMEM)] * 6,
        out_specs=[pl.BlockSpec(memory_space=pltpu.VMEM)] * 4,
        scratch_shapes=scratch,
        compiler_params=pltpu.CompilerParams(
            collective_id=1, has_side_effects=True, vmem_limit_bytes=60 * 2**20
        ),
        cost_estimate=pl.CostEstimate(flops=10**10, bytes_accessed=12 * 2**20, transcendentals=6 * 10**6),
    )(lengths, q_rows, k_rows, v_rows, do_rows, x_rows)


def local(queries, keys, values, out_grad, layer_input, doc_lengths):
    outs = fused(doc_lengths, queries[0], keys[0], values[0], out_grad[0], layer_input[0])
    return (outs[0][None], outs[1][None], outs[2][None], outs[3])


def solution(mesh):
    placed = (
        P("dp", "ctx", None),
        P("dp", "ctx", None),
        P("dp", "ctx", None),
        P("dp", "ctx", None),
        P("dp", "ctx", None),
        P("dp", None),
    )
    return jax.shard_map(
        local,
        mesh=mesh,
        in_specs=placed,
        out_specs=(
            P("dp", "ctx", None),
            P("dp", "ctx", None),
            P("dp", "ctx", None),
            P(("dp", "ctx"), None),
        ),
        check_vma=False,
    )
```

time: 309 us -> 123 us (0.40)
  waiting for transfers between devices: 124 us -> 0 us
  matrix products: 61.5 us -> 0 us
  Pallas kernels: 59.2 us -> 116 us
  local copies, waits for them, and re-layouts: 38.6 us -> 5.44 us
  starting transfers between devices: 12.7 us -> 0 us
  other arithmetic: 10.9 us -> 0 us
    ppermute x4 -> x0, waiting for transfers between devices: 124 us -> none  [shifted(): return lax.ppermute(block, axis, route)]
    dot_general x48 -> x0, matrix products: 61.5 us -> none  [the longest x8 15.9 us: group_grads(): jnp.einsum('sed,wd->esw', do_group, v_group, preferred_element_type=jnp.f...]
    pallas_call x1, Pallas kernels: 59.2 us -> 116 us  [fused(): pl.pallas_call(fused_kernel, out_shape=(jax.ShapeDtypeStruct((256, 4096),...]
    ppermute x4 -> x0, starting transfers between devices: 12.7 us -> none  [shifted(): return lax.ppermute(block, axis, route)]
    another operation x5 -> x0, local copies, waits for them, and re-layouts: 10.1 us -> none  [the longest x2 4.18 us: local(): jnp.stack((dk_window[(REACH - step) * rows:(REACH - step + 1) * rows], dv...]
    dynamic_slice x8 -> x0, local copies, waits for them, and re-layouts: 8.51 us -> none  [group_grads(): lax.dynamic_slice_in_dim(do_rows, group * (GROUP * HD), GROUP * HD, 1)]
    dynamic_update_slice x16 -> x0, local copies, waits for them, and re-layouts: 6.93 us -> none  [group_grads(): lax.dynamic_update_slice_in_dim(dq_acc, dq_group.reshape(rows, GROUP * HD...]
    reduce_sum x8 -> x0, other arithmetic: 5.45 us -> none  [group_grads(): jnp.sum(jnp.where(live, jnp.exp(scores - top), 0.0), axis=-1, keepdims=True)]
  transfers between devices with their start and end apart: 4 -> 0, of which waited for: 4 -> 0; matrix products, arithmetic and copies ran while one was open for 3% -> 0% of each run, Pallas kernels for 0% -> 0%
where the time goes in v2:
time: 123 us; the launch traced here: 122 us
  Pallas kernels  116 us (94%)
  local copies, waits for them, and re-layouts  5.44 us (4%)
    pallas_call x1, Pallas kernels, fused(): pl.pallas_call(fused_kernel, out_shape=(jax.ShapeDtypeStruct((256, 4096),...  116 us
    unnamed x10, local copies, waits for them, and re-layouts  5.44 us

profile of v2, /device:TPU:32, one launch (start us, length us, event | category | flops | bytes accessed | tf_op | source)
XLA Modules:
  0.0 121.8 jit_solution(17740513001021925771)
XLA Ops:
  0.6 115.7 %shard_map.93 = (bf16[256,4096]{1,0:T(8,128)(2,1)}, bf16[256,1024]{1,0:T(8,128)(2,1)}, bf16[256,1024]{1,0:T(8,128)(2,1)}, f32[16,1024]{1,0:T(8,128)}) custom-call(s32[1,64]{1,0:T(1,128)} %lengths_ref.1, bf16[256,4096]{1,0:T(8,128)(2,1)} %bitcast.11, bf16[256,1024]{1,0:T(8,128)(2,1)} %bitcast.14, bf16[256,1024]{1,0:T(8,128)(2,1)} %bitcast.15, ...), custom_call_target="tpu_custom_call" | custom-call | flops 10000000000 | bytes 12582912 | tf_op jit(solution)/shard_map/pallas_call | solution.py:372
  116.4 0.0 copy-start.1
  116.4 0.0 copy-start
  116.4 3.2 %copy.14 = bf16[1,256,4096]{2,1,0:T(8,128)(2,1)} copy(bf16[1,256,4096]{2,1,0:T(8,128)(2,1)} %bitcast.8) | data formatting | bytes 4194304
  119.6 0.0 copy-done.1
  119.6 0.0 copy-start.2
  119.6 0.8 copy.15
  120.4 0.0 copy-done
  120.4 0.8 copy.16
  121.2 0.0 copy-done.2
  121.2 0.6 copy.17
Async XLA Ops:
  116.4 3.2 %copy-start.1 = (bf16[256,1024]{1,0:T(8,128)(2,1)S(1)}, bf16[256,1024]{1,0:T(8,128)(2,1)}, u32[]{:S(2)}) copy-start(bf16[256,1024]{1,0:T(8,128)(2,1)} %get-tuple-element.9) | copy-start | bytes 1572868
  116.4 4.0 %copy-start = (bf16[256,1024]{1,0:T(8,128)(2,1)S(1)}, bf16[256,1024]{1,0:T(8,128)(2,1)}, u32[]{:S(2)}) copy-start(bf16[256,1024]{1,0:T(8,128)(2,1)} %get-tuple-element.10) | copy-start | bytes 1572868
  119.6 1.6 %copy-start.2 = (f32[16,1024]{1,0:T(8,128)S(1)}, f32[16,1024]{1,0:T(8,128)}, u32[]{:S(2)}) copy-start(f32[16,1024]{1,0:T(8,128)} %get-tuple-element.19) | copy-start | bytes 196612

commit v3 on v2

v3 whole, which is shorter than its diff:
```python
import jax
import jax.numpy as jnp
from jax import lax
from jax.experimental import pallas as pl
from jax.experimental.pallas import tpu as pltpu
from jax.sharding import PartitionSpec as P

KVH = 8
HD = 128
GROUP = 4
LEAD = 3
LAG = 3
RS_AT = (0, 3, 6, 9, 12)
SWAP_TICK = 4
VLATE = (5, 6, 6, 7, 7, 8, 8, 9)
P2_FROM = 15
KINDS = "xyxyxyxy"
RS_LATE = 1
VMEM_MB = 48
BF = jnp.bfloat16
F32 = jnp.float32


MESH = pl.DeviceIdType.MESH
GROUPS = tuple((g * 128, 128, kind) for g, kind in enumerate(KINDS))
SIZES = {"core": 2, "y": 4, "x": 4, "z": 8}


def place():
    dp, ctx = lax.axis_index("dp"), lax.axis_index("ctx")
    return {
        "core": lax.rem(dp, 2),
        "y": lax.rem(ctx, 2) * 2 + dp // 2,
        "x": lax.rem(ctx // 2, 4),
        "z": ctx // 8,
    }


def member(here, axis, step):
    return lax.rem(here[axis] + (step + SIZES[axis]), SIZES[axis])


def at(here, axis, step):
    spot = dict(here)
    spot[axis] = member(here, axis, step)
    dp = lax.rem(spot["y"], 2) * 2 + spot["core"]
    ctx = spot["z"] * 8 + spot["x"] * 2 + spot["y"] // 2
    return (dp, ctx)


def push(src, dst, sems, slot, target):
    copy = pltpu.make_async_remote_copy(
        src_ref=src,
        dst_ref=dst,
        send_sem=sems.at[0, slot],
        recv_sem=sems.at[1, slot],
        device_id=target,
        device_id_type=MESH,
    )
    copy.start()
    return copy


def ring(here, axis, term, keep, out, inn, sems):
    half = SIZES[axis] // 2
    count = out.shape[2]
    mid = count // 2
    ends = (at(here, axis, 1), at(here, axis, -1))
    far = term(member(here, axis, half)).astype(BF)
    copies = [[], []]
    for way in range(2):
        part = pl.ds(way * mid, mid)
        out[way, 0, part] = far[way * mid : (way + 1) * mid]
        copies[way].append(push(out.at[way, 0, part], inn.at[way, 0, part], sems, way, ends[way]))
    yield
    for step in range(1, half):
        for way in range(2):
            mine = term(member(here, axis, (half - step) * (1 - 2 * way)))
            copies[way][-1].wait_recv()
            if step == 1:
                got, rest = slice(way * mid, (way + 1) * mid), slice((1 - way) * mid, (2 - way) * mid)
                out[way, 1, got] = (mine[got] + inn[way, 0, got].astype(F32)).astype(BF)
                out[way, 1, rest] = mine[rest].astype(BF)
            else:
                out[way, step] = (mine + inn[way, step - 1].astype(F32)).astype(BF)
            copies[way].append(push(out.at[way, step], inn.at[way, step], sems, 2 * step + way, ends[way]))
        yield
    mine = term(here[axis])
    copies[0][-1].wait_recv()
    copies[1][-1].wait_recv()
    keep(mine + inn[0, half - 1].astype(F32) + inn[1, half - 1].astype(F32))
    for copy in copies[0] + copies[1]:
        copy.wait_send()


def direct(here, axis, term, keep, out, inn, sems, base):
    size = SIZES[axis]
    copies = []
    for step in sorted(range(1, size), key=lambda step: -min(step, size - step)):
        out[step - 1] = term(member(here, axis, step)).astype(BF)
        copies.append(push(out.at[step - 1], inn.at[step - 1], sems, base + step - 1, at(here, axis, step)))
    yield
    value = term(here[axis])
    for copy in copies:
        copy.wait_recv()
    for step in range(size - 1):
        value = value + inn[step].astype(F32)
    keep(value)
    for copy in copies:
        copy.wait_send()


def scatter_group(here, xt, dvg, out_ref, c0, width, first, big_out, big_in, small_out, small_in, mid_sum, low_sum, last_out, last_in, sems):
    def pieces(axis, index):
        if axis == "x":
            return xt[:, :, index].reshape(512, 512)
        return xt[lax.rem(index, 2), :, :, index // 2].reshape(512, 512)

    def product(index):
        return jnp.dot(pieces(first, index), dvg[:, c0 : c0 + width], preferred_element_type=F32)

    def middle(index):
        part = mid_sum[:, index] if first == "y" else mid_sum[lax.rem(index, 2), :, index // 2]
        return part.reshape(128, width)

    def low(index):
        return low_sum[index]

    def keep_mid(value):
        mid_sum[...] = value.reshape(mid_sum.shape)

    def keep_low(value):
        low_sum[...] = value.reshape(low_sum.shape)

    def keep_out(value):
        out_ref[:, c0 : c0 + width] = value

    yield from ring(here, first, product, keep_mid, big_out, big_in, sems)
    yield from direct(here, "x" if first == "y" else "y", middle, keep_low, small_out, small_in, sems, 4)
    yield from direct(here, "z", low, keep_out, last_out, last_in, sems, 7)


def group_scratch(width, first):
    mid = (8, 4, 16) if first == "y" else (2, 8, 2, 16)
    return [
        pltpu.VMEM((2, 2, 512, width), BF),
        pltpu.VMEM((2, 2, 512, width), BF),
        pltpu.VMEM((3, 128, width), BF),
        pltpu.VMEM((3, 128, width), BF),
        pltpu.VMEM((*mid, width), F32),
        pltpu.VMEM((8, 16, width), F32),
        pltpu.VMEM((7, 16, width), BF),
        pltpu.VMEM((7, 16, width), BF),
        pltpu.SemaphoreType.DMA((2, 14)),
    ]


SPAN = 640
HALF = 128
SCALE = HD ** (-0.5)


def dot_nt(left, right):
    return lax.dot_general(left, right, (((1,), (1,)), ((), ())), preferred_element_type=F32)


def dot_nn(left, right):
    return jnp.dot(left, right, preferred_element_type=F32)


def head_columns(head, count=1):
    return pl.ds(pl.multiple_of(head * HD, HD), count * HD)


def stacked(ref, g, half):
    rows = pl.ds(half * HALF, HALF)
    return jnp.concatenate([ref[rows, head_columns(g * GROUP + e)] for e in range(GROUP)], axis=0)


def fill_bias(lengths_ref, slab, bias):
    row = lax.broadcasted_iota(jnp.int32, (64, 64), 0)
    col = lax.broadcasted_iota(jnp.int32, (64, 64), 1)
    sizes = jnp.broadcast_to(lengths_ref[...], (64, 64))
    starts = jnp.sum(jnp.where(col < row, sizes, 0), axis=1, keepdims=True)
    for half in range(2):
        base = slab * 256 + half * HALF
        query = base + lax.broadcasted_iota(jnp.int32, (64, HALF), 1)
        first = jnp.max(jnp.where(starts <= query, starts, 0), axis=0, keepdims=True)
        key = base - 512 + lax.broadcasted_iota(jnp.int32, (SPAN, HALF), 0)
        query = base + lax.broadcasted_iota(jnp.int32, (SPAN, HALF), 1)
        value = jnp.where((key <= query) & (key >= first), 0.0, -1e30)
        for e in range(GROUP):
            bias[half, :, e * HALF : (e + 1) * HALF] = value


def probs_step(g, q_ref, do_ref, kwin, bias, pbuf, dvwin):
    for half in range(2):
        rows = pl.ds(half * HALF, SPAN)
        scores = dot_nt(kwin[g, rows], stacked(q_ref, g, half)) * (SCALE * 1.4426950408889634) + bias[half]
        top = jnp.max(scores, axis=0, keepdims=True)
        weights = jnp.exp2(scores - top)
        probs = (weights * (1.0 / jnp.sum(weights, axis=0, keepdims=True))).astype(BF)
        pbuf[g, half] = probs
        term = dot_nn(probs, stacked(do_ref, g, half))
        if half == 0:
            dvwin[0:SPAN] = term
            dvwin[SPAN:768] = jnp.zeros((HALF, HD), F32)
        else:
            dvwin[rows] += term


def grads_step(g, q_ref, do_ref, kwin, vwin, pbuf, dkwin, dq_ref):
    turned = kwin[g].T
    for half in range(2):
        rows = pl.ds(half * HALF, SPAN)
        probs = pbuf[g, half].astype(F32)
        dprobs = dot_nt(vwin[g, rows], stacked(do_ref, g, half))
        delta = jnp.sum(probs * dprobs, axis=0, keepdims=True)
        dscores = (probs * (dprobs - delta)).astype(BF)
        term = dot_nn(dscores, stacked(q_ref, g, half))
        if half == 0:
            dkwin[0:SPAN] = term
            dkwin[SPAN:768] = jnp.zeros((HALF, HD), F32)
        else:
            dkwin[rows] += term
        dq = dot_nn(turned[:, half * HALF : half * HALF + SPAN], dscores) * SCALE
        for e in range(GROUP):
            dq_ref[pl.ds(half * HALF, HALF), head_columns(g * GROUP + e)] = dq[:, e * HALF : (e + 1) * HALF].T.astype(BF)


def fused_kernel(lengths_hbm, q_hbm, k_hbm, v_hbm, do_hbm, x_hbm, dq_ref, dk_ref, dv_ref, dw_ref,
                 lengths_ref, q_ref, do_ref, x_ref, kwin, vwin, bias, pbuf, window, out1, in1, out2, in2, final,
                 xrecv, dvg, xt, load_sems, slab_sems, halo_sems, pair_sems, *scratch):
    here = place()
    dp, ctx = lax.axis_index("dp"), lax.axis_index("ctx")
    odd = lax.rem(ctx, 2)
    twin = (dp, ctx + 1 - 2 * odd)
    ahead, behind = (dp, lax.rem(ctx + 2, 64)), (dp, lax.rem(ctx + 62, 64))
    partner = at(here, "core", 1)
    relay = pl.multiple_of(512 * (1 - odd), 256)

    def link(src, dst, kind, g, target):
        return pltpu.make_async_remote_copy(
            src_ref=src, dst_ref=dst, send_sem=halo_sems.at[0, kind, g], recv_sem=halo_sems.at[1, kind, g],
            device_id=target, device_id_type=MESH)

    def halo_x(which, g):
        win = (kwin, vwin)[which]
        return link(win.at[g, pl.ds(512, 256)], win.at[g, pl.ds(0, 256)], 2 * which, g, ahead)

    def halo_y(which, g):
        win = (kwin, vwin)[which]
        return link(win.at[g, pl.ds(relay, 256)], win.at[g, pl.ds(256, 256)], 2 * which + 1, g, twin)

    def back_y(which, g):
        return link(out1.at[which, g], in1.at[which, g], 4 + 2 * which, g, twin)

    def back_x(which, g):
        return link(out2.at[which, g], in2.at[which, g], 5 + 2 * which, g, behind)

    def relayed(which, g):
        @pl.when(odd == 1)
        def _():
            halo_x(which, g).wait_recv()
            halo_y(which, g).start()

    def own_first(which, g):
        @pl.when(odd == 0)
        def _():
            halo_y(which, g).start()

    def arrived(which, g):
        halo_y(which, g).wait_recv()

        @pl.when(odd == 0)
        def _():
            halo_x(which, g).wait_recv()

    def give_near(which, g):
        out1[which, g] = window[256:512].astype(BF)
        back_y(which, g).start()
        final[which, g] = window[512:768]
        out2[which, g] = window[0:256].astype(BF)

    def give_far(which, g):
        back_y(which, g).wait_recv()
        got = in1[which, g].astype(F32)
        out2[which, g] = (out2[which, g].astype(F32) + jnp.where(odd == 1, got, 0.0)).astype(BF)
        back_x(which, g).start()
        final[which, g] += jnp.where(odd == 1, 0.0, got)

    def finish(which, g):
        back_x(which, g).wait_recv()
        total = final[which, g] + in2[which, g].astype(F32)
        if which == 0:
            dk_ref[:, head_columns(g)] = (total * SCALE).astype(BF)
        else:
            rounded = total.astype(BF)
            dv_ref[:, head_columns(g)] = rounded
            dvg[0:256, head_columns(g)] = rounded

    shares = {}

    def share(g):
        columns = pl.ds(g * HD, HD)
        shares[g] = push(dvg.at[pl.ds(0, 256), columns], dvg.at[pl.ds(256, 256), columns], pair_sems, 2 + g, partner)

    loads = [
        pltpu.make_async_copy(src, dst, load_sems.at[i])
        for i, (src, dst) in enumerate(((lengths_hbm, lengths_ref), (x_hbm, x_ref), (q_hbm, q_ref), (do_hbm, do_ref)))
    ]
    slabs = [
        [
            pltpu.make_async_copy(src.at[:, pl.ds(g * HD, HD)], win.at[g, pl.ds(512, 256)], slab_sems.at[which, g])
            for g in range(KVH)
        ]
        for which, (src, win) in enumerate(((k_hbm, kwin), (v_hbm, vwin)))
    ]
    for slab in slabs[0]:
        slab.start()
    for load in loads:
        load.start()
    for slab in slabs[1]:
        slab.start()
    greeted = [partner, ahead, behind]
    greeted += [at(here, axis, step) for axis in "xyz" for step in range(1, SIZES[axis])]
    barrier = pltpu.get_barrier_semaphore()
    for target in greeted:
        pl.semaphore_signal(barrier, inc=1, device_id=target, device_id_type=MESH)
    pl.semaphore_wait(barrier, len(greeted))
    for g in range(KVH):
        slabs[0][g].wait()
        halo_x(0, g).start()
        own_first(0, g)
    mine, other = here["core"] * 1024, (1 - here["core"]) * 1024
    loads[0].wait()
    loads[1].wait()
    swaps = []
    for part in range(2):
        columns = pl.ds(pl.multiple_of(part * 2048 + other, 128), 1024)
        swaps.append(push(x_ref.at[:, columns], xrecv.at[:, pl.ds(part * 1024, 1024)], pair_sems, part, partner))
    for slab in slabs[1]:
        slab.wait()
    fill_bias(lengths_ref, ctx, bias)
    for g in range(LEAD):
        relayed(0, g)
    for part in range(2):
        def own(z, carry):
            columns = pl.ds(pl.multiple_of(part * 2048 + mine + z * 128, 128), 128)
            xt[part, z, :, :, :, 0:256] = x_ref[:, columns].T.reshape(4, 2, 16, 256)
            return carry
        lax.fori_loop(0, 8, own, 0)
    loads[2].wait()
    loads[3].wait()

    groups = {}
    for tick in range(max(P2_FROM + KVH + 2 * LAG, 2 * LAG + KVH + RS_LATE + RS_AT[-1])):
        if tick < KVH:
            halo_x(1, tick).start()
        for g in range(KVH):
            if VLATE[g] == tick:
                own_first(1, g)
                relayed(1, g)
        if tick + LEAD < KVH:
            relayed(0, tick + LEAD)
        if tick < KVH:
            arrived(0, tick)
            probs_step(tick, q_ref, do_ref, kwin, bias, pbuf, window)
            give_near(1, tick)
        elif P2_FROM <= tick < P2_FROM + KVH:
            arrived(1, tick - P2_FROM)
            grads_step(tick - P2_FROM, q_ref, do_ref, kwin, vwin, pbuf, window, dq_ref)
            give_near(0, tick - P2_FROM)
        if tick == SWAP_TICK:
            swaps[0].wait()
            swaps[1].wait()
            for part in range(2):
                def got(z, carry):
                    columns = pl.ds(pl.multiple_of(part * 1024 + z * 128, 128), 128)
                    xt[part, z, :, :, :, 256:512] = xrecv[:, columns].T.reshape(4, 2, 16, 256)
                    return carry
                lax.fori_loop(0, 8, got, 0)
        for which in (1, 0):
            g = tick - (1 - which) * P2_FROM - LAG
            if 0 <= g < KVH:
                give_far(which, g)
            if 0 <= g - LAG < KVH:
                finish(which, g - LAG)
                if which == 1:
                    share(g - LAG)
        for i in range(KVH):
            since = tick - (2 * LAG + i + RS_LATE)
            if since == 0:
                shares[i].wait()
                c0, width, first = GROUPS[i]
                groups[i] = scatter_group(here, xt, dvg, dw_ref, c0, width, first, *scratch[i * 9 : (i + 1) * 9])
            if since in RS_AT and i in groups:
                next(groups[i], None)
    for which in range(2):
        for g in range(KVH):
            halo_x(which, g).wait_send()
            halo_y(which, g).wait_send()
            back_y(which, g).wait_send()
            back_x(which, g).wait_send()


def fused(lengths, q_rows, k_rows, v_rows, do_rows, x_rows):
    scratch = [
        pltpu.VMEM((1, 64), jnp.int32),
        pltpu.VMEM((256, 4096), BF),
        pltpu.VMEM((256, 4096), BF),
        pltpu.VMEM((256, 4096), BF),
        pltpu.VMEM((KVH, 768, HD), BF),
        pltpu.VMEM((KVH, 768, HD), BF),
        pltpu.VMEM((2, SPAN, GROUP * HALF), F32),
        pltpu.VMEM((KVH, 2, SPAN, GROUP * HALF), BF),
        pltpu.VMEM((768, HD), F32),
        pltpu.VMEM((2, KVH, 256, HD), BF),
        pltpu.VMEM((2, KVH, 256, HD), BF),
        pltpu.VMEM((2, KVH, 256, HD), BF),
        pltpu.VMEM((2, KVH, 256, HD), BF),
        pltpu.VMEM((2, KVH, 256, HD), F32),
        pltpu.VMEM((256, 2048), BF),
        pltpu.VMEM((512, 1024), BF),
        pltpu.VMEM((2, 8, 4, 2, 16, 512), BF),
        pltpu.SemaphoreType.DMA((4,)),
        pltpu.SemaphoreType.DMA((2, KVH)),
        pltpu.SemaphoreType.DMA((2, 8, KVH)),
        pltpu.SemaphoreType.DMA((2, 10)),
    ]
    for _, width, first in GROUPS:
        scratch += group_scratch(width, first)
    vmem, hbm = pl.BlockSpec(memory_space=pltpu.VMEM), pl.BlockSpec(memory_space=pltpu.HBM)
    return pl.pallas_call(
        fused_kernel,
        out_shape=(
            jax.ShapeDtypeStruct((256, 4096), BF),
            jax.ShapeDtypeStruct((256, 1024), BF),
            jax.ShapeDtypeStruct((256, 1024), BF),
            jax.ShapeDtypeStruct((16, 1024), F32),
        ),
        in_specs=[hbm] * 6,
        out_specs=[vmem] * 4,
        scratch_shapes=scratch,
        compiler_params=pltpu.CompilerParams(
            collective_id=1, has_side_effects=True, vmem_limit_bytes=VMEM_MB * 2**20
        ),
        cost_estimate=pl.CostEstimate(flops=10**10, bytes_accessed=12 * 2**20, transcendentals=6 * 10**6),
    )(lengths, q_rows, k_rows, v_rows, do_rows, x_rows)


def store_kernel(*refs):
    copies = [pltpu.make_async_copy(refs[i], refs[4 + i], refs[8].at[i]) for i in range(4)]
    for copy in copies:
        copy.start()
    for copy in copies:
        copy.wait()


def store(outs):
    return pl.pallas_call(
        store_kernel,
        out_shape=tuple(jax.ShapeDtypeStruct(out.shape, out.dtype) for out in outs),
        in_specs=[pl.BlockSpec(memory_space=pl.ANY)] * 4,
        out_specs=[pl.BlockSpec(memory_space=pltpu.HBM)] * 4,
        scratch_shapes=[pltpu.SemaphoreType.DMA((4,))],
        compiler_params=pltpu.CompilerParams(vmem_limit_bytes=2**20),
    )(*outs)


def local(queries, keys, values, out_grad, layer_input, doc_lengths):
    rows = (doc_lengths, queries[0], keys[0], values[0], out_grad[0], layer_input[0])
    outs = store(fused(*[pltpu.with_memory_space_constraint(part, pltpu.HBM) for part in rows]))
    return (outs[0][None], outs[1][None], outs[2][None], outs[3])


def solution(mesh):
    placed = (
        P("dp", "ctx", None),
        P("dp", "ctx", None),
        P("dp", "ctx", None),
        P("dp", "ctx", None),
        P("dp", "ctx", None),
        P("dp", None),
    )
    return jax.shard_map(
        local,
        mesh=mesh,
        in_specs=placed,
        out_specs=(
            P("dp", "ctx", None),
            P("dp", "ctx", None),
            P("dp", "ctx", None),
            P(("dp", "ctx"), None),
        ),
        check_vma=False,
    )
```

time: 123 us -> 98 us (0.80)
  Pallas kernels: 116 us -> 95.6 us
  local copies, waits for them, and re-layouts: 5.44 us -> 0 us
    pallas_call x1, Pallas kernels: 116 us -> 93.9 us  [fused(): pl.pallas_call(fused_kernel, out_shape=(jax.ShapeDtypeStruct((256, 4096),...]
    unnamed x10 -> x0, local copies, waits for them, and re-layouts: 5.44 us -> none
    pallas_call x0 -> x1, Pallas kernels: none -> 1.7 us  [store(): pl.pallas_call(store_kernel, out_shape=tuple((jax.ShapeDtypeStruct(out.sh...]
where the time goes in v3:
time: 98 us; the launch traced here: 96.5 us
  Pallas kernels  95.6 us (98%)
    pallas_call x1, Pallas kernels, fused(): pl.pallas_call(fused_kernel, out_shape=(jax.ShapeDtypeStruct((256, 4096),...  93.9 us

profile of v3, /device:TPU:32, one launch (start us, length us, event | category | flops | bytes accessed | tf_op | source)
XLA Modules:
  0.0 96.5 jit_solution(14755733135206045856)
XLA Ops:
  0.6 93.9 %shard_map.93 = (bf16[256,4096]{1,0:T(8,128)(2,1)S(1)}, bf16[256,1024]{1,0:T(8,128)(2,1)S(1)}, bf16[256,1024]{1,0:T(8,128)(2,1)S(1)}, f32[16,1024]{1,0:T(8,128)S(1)}) custom-call(s32[1,64]{1,0:T(1,128)} %lengths_hbm.1, bf16[256,4096]{1,0:T(8,128)(2,1)} %bitcast.8, bf16[256,1024]{1,0:T(8,128)(2,1)} %bitcast.12, bf16[256,1024]{1,0:T(8,128)(2,1)} %bitcast.13, ...), custom_call_target="tpu_custom_call" | custom-call | flops 10000000000 | bytes 12582912 | tf_op jit(solution)/shard_map/pallas_call | solution.py:434
  94.6 1.7 %shard_map.94 = (bf16[256,4096]{1,0:T(8,128)(2,1)}, bf16[256,1024]{1,0:T(8,128)(2,1)}, bf16[256,1024]{1,0:T(8,128)(2,1)}, f32[16,1024]{1,0:T(8,128)}) custom-call(bf16[256,4096]{1,0:T(8,128)(2,1)S(1)} %get-tuple-element.12.refs_0_, bf16[256,1024]{1,0:T(8,128)(2,1)S(1)} %get-tuple-element.13.refs_1_, bf16[256,1024]{1,0:T(8,128)(2,1)S(1)} %get-tuple-element.14.refs_2_, ...), custom_call_target="tpu_custom_call" | custom-call | tf_op jit(solution)/shard_map/pallas_call | solution.py:461

commit v4 on v3

--- a/solution.py
+++ b/solution.py
@@ -10,11 +10,11 @@
 GROUP = 4
 LEAD = 3
 LAG = 3
-RS_AT = (0, 3, 6, 9, 12)
+RS_AT = {"x": (0, 3, 6, 9, 12), "z": (0, 2, 5, 8, 11, 14, 17)}
 SWAP_TICK = 4
 VLATE = (5, 6, 6, 7, 7, 8, 8, 9)
 P2_FROM = 15
-KINDS = "xyxyxyxy"
+KINDS = "zzxzxzxx"
 RS_LATE = 1
 VMEM_MB = 48
 BF = jnp.bfloat16
@@ -111,20 +111,19 @@
 
 
 def scatter_group(here, xt, dvg, out_ref, c0, width, first, big_out, big_in, small_out, small_in, mid_sum, low_sum, last_out, last_in, sems):
-    def pieces(axis, index):
-        if axis == "x":
-            return xt[:, :, index].reshape(512, 512)
-        return xt[lax.rem(index, 2), :, :, index // 2].reshape(512, 512)
+    def pieces(index):
+        return xt[:, index].reshape(256, 512) if first == "z" else xt[:, :, index].reshape(512, 512)
 
     def product(index):
-        return jnp.dot(pieces(first, index), dvg[:, c0 : c0 + width], preferred_element_type=F32)
+        return jnp.dot(pieces(index), dvg[:, c0 : c0 + width], preferred_element_type=F32)
 
     def middle(index):
-        part = mid_sum[:, index] if first == "y" else mid_sum[lax.rem(index, 2), :, index // 2]
-        return part.reshape(128, width)
+        if first == "z":
+            return mid_sum[:, index].reshape(64, width)
+        return mid_sum[lax.rem(index, 2), :, index // 2].reshape(128, width)
 
     def low(index):
-        return low_sum[index]
+        return low_sum[lax.rem(index, 2), index // 2] if first == "z" else low_sum[index]
 
     def keep_mid(value):
         mid_sum[...] = value.reshape(mid_sum.shape)
@@ -136,22 +135,25 @@
         out_ref[:, c0 : c0 + width] = value
 
     yield from ring(here, first, product, keep_mid, big_out, big_in, sems)
-    yield from direct(here, "x" if first == "y" else "y", middle, keep_low, small_out, small_in, sems, 4)
-    yield from direct(here, "z", low, keep_out, last_out, last_in, sems, 7)
+    yield from direct(here, "x" if first == "z" else "y", middle, keep_low, small_out, small_in, sems, 8)
+    yield from direct(here, "y" if first == "z" else "z", low, keep_out, last_out, last_in, sems, 11)
 
 
 def group_scratch(width, first):
-    mid = (8, 4, 16) if first == "y" else (2, 8, 2, 16)
+    if first == "z":
+        big, small, last, mid, low = (4, 256), 64, 3, (2, 4, 32), (2, 2, 16)
+    else:
+        big, small, last, mid, low = (2, 512), 128, 7, (2, 8, 2, 16), (8, 16)
     return [
-        pltpu.VMEM((2, 2, 512, width), BF),
-        pltpu.VMEM((2, 2, 512, width), BF),
-        pltpu.VMEM((3, 128, width), BF),
-        pltpu.VMEM((3, 128, width), BF),
+        pltpu.VMEM((2, *big, width), BF),
+        pltpu.VMEM((2, *big, width), BF),
+        pltpu.VMEM((3, small, width), BF),
+        pltpu.VMEM((3, small, width), BF),
         pltpu.VMEM((*mid, width), F32),
-        pltpu.VMEM((8, 16, width), F32),
-        pltpu.VMEM((7, 16, width), BF),
-        pltpu.VMEM((7, 16, width), BF),
-        pltpu.SemaphoreType.DMA((2, 14)),
+        pltpu.VMEM((*low, width), F32),
+        pltpu.VMEM((last, 16, width), BF),
+        pltpu.VMEM((last, 16, width), BF),
+        pltpu.SemaphoreType.DMA((2, 18)),
     ]
 
 
@@ -354,7 +356,7 @@
     loads[3].wait()
 
     groups = {}
-    for tick in range(max(P2_FROM + KVH + 2 * LAG, 2 * LAG + KVH + RS_LATE + RS_AT[-1])):
+    for tick in range(max(P2_FROM + KVH + 2 * LAG, 2 * LAG + KVH + RS_LATE + 17)):
         if tick < KVH:
             halo_x(1, tick).start()
         for g in range(KVH):
@@ -394,7 +396,7 @@
                 shares[i].wait()
                 c0, width, first = GROUPS[i]
                 groups[i] = scatter_group(here, xt, dvg, dw_ref, c0, width, first, *scratch[i * 9 : (i + 1) * 9])
-            if since in RS_AT and i in groups:
+            if since in RS_AT[KINDS[i]]:
                 next(groups[i], None)
     for which in range(2):
         for g in range(KVH):

time: 98 us -> 94.3 us (0.962); the launches traced: 96.5 us -> 94.1 us
  Pallas kernels: 95.6 us -> 93.2 us
    pallas_call x1, Pallas kernels: 93.9 us -> 91.5 us  [fused(): pl.pallas_call(fused_kernel, out_shape=(jax.ShapeDtypeStruct((256, 4096),...]
where the time goes in v4:
time: 94.3 us; the launch traced here: 94.1 us
  Pallas kernels  93.2 us (99%)
    pallas_call x1, Pallas kernels, fused(): pl.pallas_call(fused_kernel, out_shape=(jax.ShapeDtypeStruct((256, 4096),...  91.5 us

profile of v4, /device:TPU:32, one launch (start us, length us, event | category | flops | bytes accessed | tf_op | source)
XLA Modules:
  0.0 94.1 jit_solution(16216623082166669694)
XLA Ops:
  0.6 91.5 %shard_map.93 = (bf16[256,4096]{1,0:T(8,128)(2,1)S(1)}, bf16[256,1024]{1,0:T(8,128)(2,1)S(1)}, bf16[256,1024]{1,0:T(8,128)(2,1)S(1)}, f32[16,1024]{1,0:T(8,128)S(1)}) custom-call(s32[1,64]{1,0:T(1,128)} %lengths_hbm.1, bf16[256,4096]{1,0:T(8,128)(2,1)} %bitcast.8, bf16[256,1024]{1,0:T(8,128)(2,1)} %bitcast.12, bf16[256,1024]{1,0:T(8,128)(2,1)} %bitcast.13, ...), custom_call_target="tpu_custom_call" | custom-call | flops 10000000000 | bytes 12582912 | tf_op jit(solution)/shard_map/pallas_call | solution.py:436
  92.2 1.7 %shard_map.94 = (bf16[256,4096]{1,0:T(8,128)(2,1)}, bf16[256,1024]{1,0:T(8,128)(2,1)}, bf16[256,1024]{1,0:T(8,128)(2,1)}, f32[16,1024]{1,0:T(8,128)}) custom-call(bf16[256,4096]{1,0:T(8,128)(2,1)S(1)} %get-tuple-element.12.refs_0_, bf16[256,1024]{1,0:T(8,128)(2,1)S(1)} %get-tuple-element.13.refs_1_, bf16[256,1024]{1,0:T(8,128)(2,1)S(1)} %get-tuple-element.14.refs_2_, ...), custom_call_target="tpu_custom_call" | custom-call | tf_op jit(solution)/shard_map/pallas_call | solution.py:463
